TPU v7x, 32 devices: a whole 2x2x4 slice. The times are simulated.
32 devices in a mesh: grp: 2 (over x), feed: 16 (over z, y, core).
Axes of the slice: x: 2, y: 2, z: 4, core: 2. Of those that a mesh axis runs over, the one named last changes fastest.
Arguments:
- samples: bfloat16 [32, 256, 65536], P(('grp', 'feed')), parts along dimension 0, may hold values from -6 to 6
- pfb_taps: float32 [4, 8192], replicated, may hold values from -0.03125 to 0.03125
Outputs:
- visibility: float32 [16384, 4096], P(('grp', 'feed')), parts along dimension 0
There are 2 independent parts, one for each index of `grp`. A program takes and returns all parts, laid end to end along the dimension named above; an argument that names none is the same for every part. Nothing has to cross between parts.
All inputs are finite; a program needn't handle non-finite values.
Results may differ from a plain program's by a relative error of at most 0.004.
Values may be sent and summed in bfloat16 or wider, within the bound.
No kernel may reach another device: no remote copies, remote signals or barrier semaphores. Data moves between devices by JAX's collectives and lax.ppermute only.
A program may use at most 192 MiB of HBM per device.

v0:
```python
import functools
import math

import jax
import jax.numpy as jnp
import numpy as np
from jax import lax
from jax.experimental import pallas as pl
from jax.experimental.pallas import tpu as pltpu
from jax.sharding import PartitionSpec as P

FIRST_CH = 1536
TIME_BLOCKS = 2
ROWS_DEV = 512
PIECES = 2
TABLE_STEP = 1024
BLOCK_ROWS = 64


def dft_rows(fft_len, first_channel, channel_count):
    sample_ids = np.arange(fft_len, dtype=np.int64)
    channel_ids = first_channel + np.arange(channel_count, dtype=np.int64)
    phase = channel_ids[:, None] * sample_ids[None, :] % fft_len
    angle = phase.astype(np.float64) * (2.0 * math.pi / fft_len)
    return np.concatenate([np.cos(angle), -np.sin(angle)], axis=0).astype(np.float32)


def spectra_kernel(owners, x_hbm, taps_ref, dft_ref, *rest):
    channels = dft_ref.shape[0] // 2
    outs, (x_buf, table, window, parts, sems) = rest[:channels], rest[channels:]
    tap_count, fft_len = taps_ref.shape
    columns = 2 * channels
    frame_count = x_hbm.shape[2] // fft_len
    piece = fft_len // PIECES
    edge = tap_count - 1
    width = tap_count * columns
    my_plane = lax.axis_index("feed") // owners
    later_block = my_plane >= channels // TIME_BLOCKS

    def fetch(index):
        span = pl.ds(pl.multiple_of(index * piece, piece), piece)
        return pltpu.make_async_copy(x_hbm.at[0, :, span], x_buf.at[:, span], sems.at[index])

    @pl.loop(0, frame_count * PIECES)
    def _(index):
        fetch(index).start()

    window[...] = jnp.zeros_like(window)

    @pl.loop(0, fft_len // TABLE_STEP)
    def _(index):
        span = pl.ds(pl.multiple_of(index * TABLE_STEP, TABLE_STEP), TABLE_STEP)
        dft = dft_ref[:, span]
        scaled = jnp.concatenate([taps_ref[m : m + 1, span] * dft for m in range(tap_count)], axis=0)
        high = scaled.astype(jnp.bfloat16).astype(jnp.float32)
        both = jnp.concatenate([high, scaled - high], axis=0)
        table[span, :] = both.T.astype(jnp.bfloat16)

    @pl.loop(0, frame_count)
    def _(frame):
        total = None
        for p in range(PIECES):
            fetch(frame * PIECES + p).wait()
            start = pl.multiple_of(frame * fft_len + p * piece, piece)
            product = jnp.dot(
                x_buf[:, pl.ds(start, piece)],
                table[p * piece : (p + 1) * piece, :],
                preferred_element_type=jnp.float32,
            )
            total = product if total is None else total + product
        turned = total.T
        summed = turned[:width] + turned[width:]
        for m in range(tap_count):
            window[frame + edge - m] += summed[m * columns : (m + 1) * columns]

    for spot in range(frame_count + edge):
        parts[:, spot, :] = window[spot]

    for k in range(channels):
        c = lax.rem(my_plane + k, channels)
        now = jnp.concatenate([parts[c, :frame_count], parts[channels + c, :frame_count]], axis=0)
        high = now.astype(jnp.bfloat16)
        low = now - high.astype(jnp.float32)
        low = jnp.concatenate([low[:4], low[frame_count : frame_count + 4]], axis=0)
        tail = jnp.concatenate(
            [parts[c, frame_count : frame_count + 4], parts[channels + c, frame_count : frame_count + 4]],
            axis=0,
        )
        sublane = lax.broadcasted_iota(jnp.int32, tail.shape, 0)
        tail = jnp.where(sublane % 4 < edge, tail, 0.0)
        tail_high = tail.astype(jnp.bfloat16).astype(jnp.float32)
        tail_low = tail - tail_high
        extra = jnp.concatenate(
            [jnp.where(later_block, low, tail_high), jnp.where(later_block, 0.0, tail_low)], axis=0
        ).astype(jnp.bfloat16)
        outs[k][...] = jnp.concatenate([high, extra], axis=0)


def join_kernel(owners, *refs):
    channels = len(refs) - 2
    out_ref, slots = refs[channels:]
    rows = slots.shape[1]
    feed_count = slots.shape[2]
    frame_count = rows // 4
    half = channels // TIME_BLOCKS
    my_plane = lax.axis_index("feed") // owners
    for k in range(channels):
        slots[lax.rem(my_plane + channels - k, channels)] = refs[k][...]
    for p in range(half):
        first = slots[p].astype(jnp.float32)
        second = slots[half + p].astype(jnp.float32)
        extra = (
            first[2 * frame_count : 3 * frame_count]
            + first[3 * frame_count :]
            + second[2 * frame_count : 3 * frame_count]
        )
        zero = jnp.zeros((frame_count - 4, feed_count), jnp.float32)
        extra = jnp.concatenate([extra[:4], zero, extra[4:8], zero], axis=0)
        fixed = second[: 2 * frame_count] + extra
        out_ref[p, : 2 * frame_count] = slots[p, : 2 * frame_count]
        out_ref[p, 2 * frame_count :] = fixed.astype(jnp.bfloat16)


def correlate_kernel(scale, owners, *refs):
    got, (out_hbm, slots, right, left, out_buf, sems) = refs[:owners], refs[owners:]
    half, rows, feed_count = got[0].shape
    frame_count = rows // 4
    total_feeds = right.shape[1]
    blocks = left.shape[0]
    block_rows = left.shape[1] // 2
    my_place = lax.axis_index("feed") % owners

    for k in range(owners):
        slots[lax.rem(my_place + owners - k, owners)] = got[k][...]
    for o in range(owners):
        for p in range(half):
            start = (p * owners + o) * feed_count
            right[:, start : start + feed_count] = slots[o, p]
    row_start = my_place * ROWS_DEV
    mine = right[:, pl.ds(pl.multiple_of(row_start, ROWS_DEV), ROWS_DEV)].astype(jnp.float32)
    halves = [mine[k * frame_count : (k + 1) * frame_count] for k in range(4)]
    swapped = jnp.concatenate([halves[1], -halves[0], halves[3], -halves[2]], axis=0)
    left[:, :block_rows, :] = mine.T.astype(jnp.bfloat16).reshape(blocks, block_rows, rows)
    left[:, block_rows:, :] = swapped.T.astype(jnp.bfloat16).reshape(blocks, block_rows, rows)

    def store(block):
        span = pl.ds(pl.multiple_of(block * block_rows, block_rows), block_rows)
        return pltpu.make_async_copy(out_buf.at[span], out_hbm.at[span], sems.at[block])

    @pl.loop(0, blocks)
    def _(block):
        product = jnp.dot(left[block], right[...], preferred_element_type=jnp.float32) * scale
        span = pl.ds(pl.multiple_of(block * block_rows, block_rows), block_rows)
        out_buf[span, :total_feeds] = product[:block_rows]
        out_buf[span, total_feeds:] = product[block_rows:]
        store(block).start()

    @pl.loop(0, blocks)
    def _(block):
        store(block).wait()


def body(samples, pfb_taps):
    feed_count = samples.shape[1]
    tap_count, fft_len = pfb_taps.shape
    frame_count = samples.shape[2] // fft_len
    devices = lax.axis_size("feed")
    total_feeds = feed_count * devices // TIME_BLOCKS
    channels = devices * ROWS_DEV // total_feeds
    owners = total_feeds // ROWS_DEV
    half = channels // TIME_BLOCKS
    spectra_count = TIME_BLOCKS * frame_count
    columns = 2 * channels
    rows = 4 * frame_count
    dft = jnp.asarray(dft_rows(fft_len, FIRST_CH, channels))
    in_vmem = pl.BlockSpec(memory_space=pltpu.VMEM)
    sent = pl.pallas_call(
        functools.partial(spectra_kernel, owners),
        out_shape=[jax.ShapeDtypeStruct((rows, feed_count), jnp.bfloat16)] * channels,
        in_specs=[pl.BlockSpec(memory_space=pl.ANY), in_vmem, in_vmem],
        out_specs=[in_vmem] * channels,
        scratch_shapes=[
            pltpu.VMEM((feed_count, samples.shape[2]), jnp.bfloat16),
            pltpu.VMEM((fft_len, 2 * tap_count * columns), jnp.bfloat16),
            pltpu.VMEM((frame_count + tap_count - 1, columns, feed_count), jnp.float32),
            pltpu.VMEM((columns, 2 * frame_count, feed_count), jnp.float32),
            pltpu.SemaphoreType.DMA((frame_count * PIECES,)),
        ],
        compiler_params=pltpu.CompilerParams(vmem_limit_bytes=56 * 2**20),
        name="spectra",
    )(samples, pfb_taps, dft)

    def to_plane(value, k):
        pairs = [
            (z * owners + q, (z + k) % channels * owners + q)
            for z in range(channels)
            for q in range(owners)
        ]
        return lax.ppermute(value, "feed", pairs)

    def to_place(value, k):
        pairs = [
            (z * owners + q, z * owners + (q + k) % owners)
            for z in range(channels)
            for q in range(owners)
        ]
        return lax.ppermute(value, "feed", pairs)

    arrived = [sent[0]] + [to_plane(sent[k], k) for k in range(1, channels)]
    joined = pl.pallas_call(
        functools.partial(join_kernel, owners),
        out_shape=jax.ShapeDtypeStruct((half, rows, feed_count), jnp.bfloat16),
        in_specs=[in_vmem] * channels,
        out_specs=in_vmem,
        scratch_shapes=[pltpu.VMEM((channels, rows, feed_count), jnp.bfloat16)],
        name="join",
    )(*arrived)
    spread = [joined] + [to_place(joined, k) for k in range(1, owners)]
    blocks = ROWS_DEV // BLOCK_ROWS
    return pl.pallas_call(
        functools.partial(correlate_kernel, 1.0 / spectra_count, owners),
        out_shape=jax.ShapeDtypeStruct((ROWS_DEV, 2 * total_feeds), jnp.float32),
        in_specs=[in_vmem] * owners,
        out_specs=pl.BlockSpec(memory_space=pl.ANY),
        scratch_shapes=[
            pltpu.VMEM((owners, half, rows, feed_count), jnp.bfloat16),
            pltpu.VMEM((rows, total_feeds), jnp.bfloat16),
            pltpu.VMEM((blocks, 2 * BLOCK_ROWS, rows), jnp.bfloat16),
            pltpu.VMEM((ROWS_DEV, 2 * total_feeds), jnp.float32),
            pltpu.SemaphoreType.DMA((blocks,)),
        ],
        compiler_params=pltpu.CompilerParams(vmem_limit_bytes=32 * 2**20),
        name="correlate",
    )(*spread)


def solution(mesh):
    placed = (P(("grp", "feed"), None, None), P())
    return jax.shard_map(
        body, mesh=mesh, in_specs=placed, out_specs=P(("grp", "feed"), None), check_vma=False
    )
```

profile of v0, /device:TPU:0, one launch (start us, length us, event | category | flops | bytes accessed | tf_op | source)
XLA Modules:
  0.0 37.6 jit_solution(5120456233519331869)
XLA Ops:
  0.0 16.3 %spectra.1 = (bf16[32,256]{1,0:T(8,128)(2,1)}, bf16[32,256]{1,0:T(8,128)(2,1)}, bf16[32,256]{1,0:T(8,128)(2,1)}, bf16[32,256]{1,0:T(8,128)(2,1)}) custom-call(bf16[1,256,65536]{2,1,0:T(8,128)(2,1)} %x_hbm.1, f32[4,8192]{1,0:T(4,128)} %taps_ref.1, f32[8,8192]{1,0:T(8,128)} %constant.2.clone.dft_ref), custom_call_target="tpu_custom_call" | custom-call | tf_op jit(solution)/shard_map/spectra/pallas_call | solution.py:177
  16.3 3.1 %collective-permute-start = (bf16[32,256]{1,0:T(8,128)(2,1)}, bf16[32,256]{1,0:T(8,128)(2,1)S(1)}, u32[]{:S(2)}, u32[]{:S(2)}) collective-permute-start(bf16[32,256]{1,0:T(8,128)(2,1)} %get-tuple-element.10), channel_id=1, source_target_pairs={{0,4},{1,5},{2,6},{3,7},{4,8},{5,9},{6,10},{7,11},{8,12},{9,13},{1... | collective-permute-start | bytes 49160 | tf_op jit(solution)/shard_map/ppermute | solution.py:199
  19.4 2.6 %collective-permute-start.1 = (bf16[32,256]{1,0:T(8,128)(2,1)}, bf16[32,256]{1,0:T(8,128)(2,1)S(1)}, u32[]{:S(2)}, u32[]{:S(2)}) collective-permute-start(bf16[32,256]{1,0:T(8,128)(2,1)} %get-tuple-element.11), channel_id=1, source_target_pairs={{0,8},{1,9},{2,10},{3,11},{4,12},{5,13},{6,14},{7,15},{8,0},{9,1},... | collective-permute-start | bytes 49160 | tf_op jit(solution)/shard_map/ppermute | solution.py:199
  22.0 1.3 %collective-permute-start.2 = (bf16[32,256]{1,0:T(8,128)(2,1)}, bf16[32,256]{1,0:T(8,128)(2,1)S(1)}, u32[]{:S(2)}, u32[]{:S(2)}) collective-permute-start(bf16[32,256]{1,0:T(8,128)(2,1)} %get-tuple-element.12), channel_id=1, source_target_pairs={{0,12},{1,13},{2,14},{3,15},{4,0},{5,1},{6,2},{7,3},{8,4},{9,5},{1... | collective-permute-start | bytes 49160 | tf_op jit(solution)/shard_map/ppermute | solution.py:199
  23.4 0.0 collective-permute-done.refs_1_
  23.4 0.0 copy-start.1
  23.4 1.0 %collective-permute-done.1.refs_2_ = bf16[32,256]{1,0:T(8,128)(2,1)S(1)} collective-permute-done((bf16[32,256]{1,0:T(8,128)(2,1)}, bf16[32,256]{1,0:T(8,128)(2,1)S(1)}, u32[]{:S(2)}, u32[]{:S(2)}) %collective-permute-start.1) | collective-permute-done | bytes 16416 | tf_op jit(solution)/shard_map/ppermute | solution.py:199
  24.4 0.0 copy-start.2
  24.4 1.6 %collective-permute-done.2.refs_3_ = bf16[32,256]{1,0:T(8,128)(2,1)S(1)} collective-permute-done((bf16[32,256]{1,0:T(8,128)(2,1)}, bf16[32,256]{1,0:T(8,128)(2,1)S(1)}, u32[]{:S(2)}, u32[]{:S(2)}) %collective-permute-start.2) | collective-permute-done | bytes 16416 | tf_op jit(solution)/shard_map/ppermute | solution.py:199
  26.0 0.0 copy-start.3
  26.0 0.0 copy-done.1
  26.0 0.0 copy-done.2
  26.0 0.6 %copy-done.3 = bf16[32,256]{1,0:T(8,128)(2,1)} copy-done((bf16[32,256]{1,0:T(8,128)(2,1)}, bf16[32,256]{1,0:T(8,128)(2,1)S(1)}, u32[]{:S(2)}) %copy-start.3) | copy-done | bytes 16408
  26.6 1.4 %join.1.refs_0_ = bf16[2,32,256]{2,1,0:T(8,128)(2,1)} custom-call(bf16[32,256]{1,0:T(8,128)(2,1)} %get-tuple-element.9.refs_0_, bf16[32,256]{1,0:T(8,128)(2,1)} %copy-done.1, bf16[32,256]{1,0:T(8,128)(2,1)} %copy-done.2, bf16[32,256]{1,0:T(8,128)(2,1)} %copy-done.3), custom_call_target="tpu_custom_call" | custom-call | tf_op jit(solution)/shard_map/join/pallas_call | solution.py:210
  28.0 0.0 collective-permute-start.5
  28.0 1.5 %collective-permute-start.4 = (bf16[2,32,256]{2,1,0:T(8,128)(2,1)}, bf16[2,32,256]{2,1,0:T(8,128)(2,1)S(1)}, u32[]{:S(2)}, u32[]{:S(2)}) collective-permute-start(bf16[2,32,256]{2,1,0:T(8,128)(2,1)} %join.1.refs_0_), channel_id=1, source_target_pairs={{0,2},{1,3},{2,0},{3,1},{4,6},{5,7},{6,4},{7,5},{8,10},{9,11},{10,... | collective-permute-start | bytes 98312 | tf_op jit(solution)/shard_map/ppermute | solution.py:207
  29.5 0.2 collective-permute-start.3
  29.7 0.2 collective-permute-done.5.refs_3_
  29.9 2.4 %collective-permute-done.4.refs_2_ = bf16[2,32,256]{2,1,0:T(8,128)(2,1)S(1)} collective-permute-done((bf16[2,32,256]{2,1,0:T(8,128)(2,1)}, bf16[2,32,256]{2,1,0:T(8,128)(2,1)S(1)}, u32[]{:S(2)}, u32[]{:S(2)}) %collective-permute-start.4) | collective-permute-done | bytes 32800 | tf_op jit(solution)/shard_map/ppermute | solution.py:207
  32.3 0.7 %collective-permute-done.3.refs_1_ = bf16[2,32,256]{2,1,0:T(8,128)(2,1)S(1)} collective-permute-done((bf16[2,32,256]{2,1,0:T(8,128)(2,1)}, bf16[2,32,256]{2,1,0:T(8,128)(2,1)S(1)}, u32[]{:S(2)}, u32[]{:S(2)}) %collective-permute-start.3) | collective-permute-done | bytes 32800 | tf_op jit(solution)/shard_map/ppermute | solution.py:207
  33.0 0.0 copy-start
  33.0 0.8 %copy-done = bf16[2,32,256]{2,1,0:T(8,128)(2,1)S(1)} copy-done((bf16[2,32,256]{2,1,0:T(8,128)(2,1)S(1)}, bf16[2,32,256]{2,1,0:T(8,128)(2,1)}, u32[]{:S(2)}) %copy-start) | copy-done | bytes 32792
  33.8 3.8 %correlate.1 = f32[512,4096]{1,0:T(8,128)} custom-call(bf16[2,32,256]{2,1,0:T(8,128)(2,1)S(1)} %copy-done, bf16[2,32,256]{2,1,0:T(8,128)(2,1)S(1)} %collective-permute-done.3.refs_1_, bf16[2,32,256]{2,1,0:T(8,128)(2,1)S(1)} %collective-permute-done.4.refs_2_, bf16[2,32,256]{2,1,0:T(8,128)(2,1)S(1)} %collective-permute-done.5.refs_3_), custom_call_target="tpu_custom_call" | custom-call | tf_op jit(solution)/shard_map/correlate/pallas_call | solution.py:220
Async XLA Ops:
  16.3 7.0 %collective-permute-start = (bf16[32,256]{1,0:T(8,128)(2,1)}, bf16[32,256]{1,0:T(8,128)(2,1)S(1)}, u32[]{:S(2)}, u32[]{:S(2)}) collective-permute-start(bf16[32,256]{1,0:T(8,128)(2,1)} %get-tuple-element.10), channel_id=1, source_target_pairs={{0,4},{1,5},{2,6},{3,7},{4,8},{5,9},{6,10},{7,11},{8,12},{9,13},{1... | collective-permute-start | bytes 49160 | tf_op jit(solution)/shard_map/ppermute | solution.py:199
  19.4 5.0 %collective-permute-start.1 = (bf16[32,256]{1,0:T(8,128)(2,1)}, bf16[32,256]{1,0:T(8,128)(2,1)S(1)}, u32[]{:S(2)}, u32[]{:S(2)}) collective-permute-start(bf16[32,256]{1,0:T(8,128)(2,1)} %get-tuple-element.11), channel_id=1, source_target_pairs={{0,8},{1,9},{2,10},{3,11},{4,12},{5,13},{6,14},{7,15},{8,0},{9,1},... | collective-permute-start | bytes 49160 | tf_op jit(solution)/shard_map/ppermute | solution.py:199
  22.0 3.9 %collective-permute-start.2 = (bf16[32,256]{1,0:T(8,128)(2,1)}, bf16[32,256]{1,0:T(8,128)(2,1)S(1)}, u32[]{:S(2)}, u32[]{:S(2)}) collective-permute-start(bf16[32,256]{1,0:T(8,128)(2,1)} %get-tuple-element.12), channel_id=1, source_target_pairs={{0,12},{1,13},{2,14},{3,15},{4,0},{5,1},{6,2},{7,3},{8,4},{9,5},{1... | collective-permute-start | bytes 49160 | tf_op jit(solution)/shard_map/ppermute | solution.py:199
  23.4 2.6 %copy-start.1 = (bf16[32,256]{1,0:T(8,128)(2,1)}, bf16[32,256]{1,0:T(8,128)(2,1)S(1)}, u32[]{:S(2)}) copy-start(bf16[32,256]{1,0:T(8,128)(2,1)S(1)} %collective-permute-done.refs_1_) | copy-start | bytes 49156
  24.4 1.6 %copy-start.2 = (bf16[32,256]{1,0:T(8,128)(2,1)}, bf16[32,256]{1,0:T(8,128)(2,1)S(1)}, u32[]{:S(2)}) copy-start(bf16[32,256]{1,0:T(8,128)(2,1)S(1)} %collective-permute-done.1.refs_2_) | copy-start | bytes 49156
  26.0 0.6 %copy-start.3 = (bf16[32,256]{1,0:T(8,128)(2,1)}, bf16[32,256]{1,0:T(8,128)(2,1)S(1)}, u32[]{:S(2)}) copy-start(bf16[32,256]{1,0:T(8,128)(2,1)S(1)} %collective-permute-done.2.refs_3_) | copy-start | bytes 49156
  28.0 1.9 %collective-permute-start.5 = (bf16[2,32,256]{2,1,0:T(8,128)(2,1)}, bf16[2,32,256]{2,1,0:T(8,128)(2,1)S(1)}, u32[]{:S(2)}, u32[]{:S(2)}) collective-permute-start(bf16[2,32,256]{2,1,0:T(8,128)(2,1)} %join.1.refs_0_), channel_id=1, source_target_pairs={{0,3},{1,0},{2,1},{3,2},{4,7},{5,4},{6,5},{7,6},{8,11},{9,8},{10,9... | collective-permute-start | bytes 98312 | tf_op jit(solution)/shard_map/ppermute | solution.py:207
  28.0 4.3 %collective-permute-start.4 = (bf16[2,32,256]{2,1,0:T(8,128)(2,1)}, bf16[2,32,256]{2,1,0:T(8,128)(2,1)S(1)}, u32[]{:S(2)}, u32[]{:S(2)}) collective-permute-start(bf16[2,32,256]{2,1,0:T(8,128)(2,1)} %join.1.refs_0_), channel_id=1, source_target_pairs={{0,2},{1,3},{2,0},{3,1},{4,6},{5,7},{6,4},{7,5},{8,10},{9,11},{10,... | collective-permute-start | bytes 98312 | tf_op jit(solution)/shard_map/ppermute | solution.py:207
  29.5 3.6 %collective-permute-start.3 = (bf16[2,32,256]{2,1,0:T(8,128)(2,1)}, bf16[2,32,256]{2,1,0:T(8,128)(2,1)S(1)}, u32[]{:S(2)}, u32[]{:S(2)}) collective-permute-start(bf16[2,32,256]{2,1,0:T(8,128)(2,1)} %join.1.refs_0_), channel_id=1, source_target_pairs={{0,1},{1,2},{2,3},{3,0},{4,5},{5,6},{6,7},{7,4},{8,9},{9,10},{10,1... | collective-permute-start | bytes 98312 | tf_op jit(solution)/shard_map/ppermute | solution.py:207
  33.0 0.8 %copy-start = (bf16[2,32,256]{2,1,0:T(8,128)(2,1)S(1)}, bf16[2,32,256]{2,1,0:T(8,128)(2,1)}, u32[]{:S(2)}) copy-start(bf16[2,32,256]{2,1,0:T(8,128)(2,1)} %join.1.refs_0_) | copy-start | bytes 98308
where the time goes:
time: 37.9 us; the launch traced here: 37.6 us
  Pallas kernels  21.5 us (57%)
  starting transfers between devices  8.76 us (23%)
  waiting for transfers between devices  5.92 us (16%)
  local copies, waits for them, and re-layouts  1.36 us (4%)
    pallas_call x1, Pallas kernels, body(): pl.pallas_call(functools.partial(spectra_kernel, owners), out_shape=[jax....  16.3 us
    ppermute x3, starting transfers between devices, to_plane(): return lax.ppermute(value, 'feed', pairs)  7.01 us
    pallas_call x1, Pallas kernels, body(): pl.pallas_call(functools.partial(correlate_kernel, 1.0 / spectra_count, o...  3.8 us
    ppermute x3, waiting for transfers between devices, to_place(): return lax.ppermute(value, 'feed', pairs)  3.32 us
    ppermute x3, waiting for transfers between devices, to_plane(): return lax.ppermute(value, 'feed', pairs)  2.59 us
    ppermute x3, starting transfers between devices, to_place(): return lax.ppermute(value, 'feed', pairs)  1.75 us
    pallas_call x1, Pallas kernels, body(): pl.pallas_call(functools.partial(join_kernel, owners), out_shape=jax.Shap...  1.4 us
    unnamed x8, local copies, waits for them, and re-layouts  1.36 us
  transfers between devices with their start and end apart: 6, of which 5 were waited for; matrix products, arithmetic and copies ran while one was open for 0% of the time, Pallas kernels for 0%

commit v1 on v0

--- a/solution.py
+++ b/solution.py
@@ -25,9 +25,10 @@
     return np.concatenate([np.cos(angle), -np.sin(angle)], axis=0).astype(np.float32)
 
 
-def spectra_kernel(owners, x_hbm, taps_ref, dft_ref, *rest):
+def spectra_kernel(
+    owners, x_hbm, taps_ref, dft_ref, out_ref, x_buf, table, window, parts, sems
+):
     channels = dft_ref.shape[0] // 2
-    outs, (x_buf, table, window, parts, sems) = rest[:channels], rest[channels:]
     tap_count, fft_len = taps_ref.shape
     columns = 2 * channels
     frame_count = x_hbm.shape[2] // fft_len
@@ -61,6 +62,7 @@
         total = None
         for p in range(PIECES):
             fetch(frame * PIECES + p).wait()
+        for p in range(PIECES):
             start = pl.multiple_of(frame * fft_len + p * piece, piece)
             product = jnp.dot(
                 x_buf[:, pl.ds(start, piece)],
@@ -76,8 +78,7 @@
     for spot in range(frame_count + edge):
         parts[:, spot, :] = window[spot]
 
-    for k in range(channels):
-        c = lax.rem(my_plane + k, channels)
+    for c in range(channels):
         now = jnp.concatenate([parts[c, :frame_count], parts[channels + c, :frame_count]], axis=0)
         high = now.astype(jnp.bfloat16)
         low = now - high.astype(jnp.float32)
@@ -93,19 +94,13 @@
         extra = jnp.concatenate(
             [jnp.where(later_block, low, tail_high), jnp.where(later_block, 0.0, tail_low)], axis=0
         ).astype(jnp.bfloat16)
-        outs[k][...] = jnp.concatenate([high, extra], axis=0)
-
-
-def join_kernel(owners, *refs):
-    channels = len(refs) - 2
-    out_ref, slots = refs[channels:]
-    rows = slots.shape[1]
-    feed_count = slots.shape[2]
+        out_ref[c] = jnp.concatenate([high, extra], axis=0)
+
+
+def join_kernel(slots, out_ref):
+    channels, rows, feed_count = slots.shape
     frame_count = rows // 4
     half = channels // TIME_BLOCKS
-    my_plane = lax.axis_index("feed") // owners
-    for k in range(channels):
-        slots[lax.rem(my_plane + channels - k, channels)] = refs[k][...]
     for p in range(half):
         first = slots[p].astype(jnp.float32)
         second = slots[half + p].astype(jnp.float32)
@@ -117,25 +112,23 @@
         zero = jnp.zeros((frame_count - 4, feed_count), jnp.float32)
         extra = jnp.concatenate([extra[:4], zero, extra[4:8], zero], axis=0)
         fixed = second[: 2 * frame_count] + extra
-        out_ref[p, : 2 * frame_count] = slots[p, : 2 * frame_count]
-        out_ref[p, 2 * frame_count :] = fixed.astype(jnp.bfloat16)
-
-
-def correlate_kernel(scale, owners, *refs):
-    got, (out_hbm, slots, right, left, out_buf, sems) = refs[:owners], refs[owners:]
-    half, rows, feed_count = got[0].shape
+        for o in range(out_ref.shape[0]):
+            out_ref[o, p, : 2 * frame_count] = slots[p, : 2 * frame_count]
+            out_ref[o, p, 2 * frame_count :] = fixed.astype(jnp.bfloat16)
+
+
+def correlate_kernel(scale, got, out_hbm, right, left, out_buf, sems):
+    owners, half, rows, feed_count = got.shape
     frame_count = rows // 4
     total_feeds = right.shape[1]
     blocks = left.shape[0]
     block_rows = left.shape[1] // 2
     my_place = lax.axis_index("feed") % owners
 
-    for k in range(owners):
-        slots[lax.rem(my_place + owners - k, owners)] = got[k][...]
     for o in range(owners):
         for p in range(half):
             start = (p * owners + o) * feed_count
-            right[:, start : start + feed_count] = slots[o, p]
+            right[:, start : start + feed_count] = got[o, p]
     row_start = my_place * ROWS_DEV
     mine = right[:, pl.ds(pl.multiple_of(row_start, ROWS_DEV), ROWS_DEV)].astype(jnp.float32)
     halves = [mine[k * frame_count : (k + 1) * frame_count] for k in range(4)]
@@ -176,9 +169,9 @@
     in_vmem = pl.BlockSpec(memory_space=pltpu.VMEM)
     sent = pl.pallas_call(
         functools.partial(spectra_kernel, owners),
-        out_shape=[jax.ShapeDtypeStruct((rows, feed_count), jnp.bfloat16)] * channels,
+        out_shape=jax.ShapeDtypeStruct((channels, rows, feed_count), jnp.bfloat16),
         in_specs=[pl.BlockSpec(memory_space=pl.ANY), in_vmem, in_vmem],
-        out_specs=[in_vmem] * channels,
+        out_specs=in_vmem,
         scratch_shapes=[
             pltpu.VMEM((feed_count, samples.shape[2]), jnp.bfloat16),
             pltpu.VMEM((fft_len, 2 * tap_count * columns), jnp.bfloat16),
@@ -190,40 +183,24 @@
         name="spectra",
     )(samples, pfb_taps, dft)
 
-    def to_plane(value, k):
-        pairs = [
-            (z * owners + q, (z + k) % channels * owners + q)
-            for z in range(channels)
-            for q in range(owners)
-        ]
-        return lax.ppermute(value, "feed", pairs)
-
-    def to_place(value, k):
-        pairs = [
-            (z * owners + q, z * owners + (q + k) % owners)
-            for z in range(channels)
-            for q in range(owners)
-        ]
-        return lax.ppermute(value, "feed", pairs)
-
-    arrived = [sent[0]] + [to_plane(sent[k], k) for k in range(1, channels)]
+    lines = [[z * owners + q for z in range(channels)] for q in range(owners)]
+    planes = [[z * owners + q for q in range(owners)] for z in range(channels)]
+    arrived = lax.all_to_all(sent, "feed", 0, 0, axis_index_groups=lines, tiled=True)
     joined = pl.pallas_call(
-        functools.partial(join_kernel, owners),
-        out_shape=jax.ShapeDtypeStruct((half, rows, feed_count), jnp.bfloat16),
-        in_specs=[in_vmem] * channels,
+        join_kernel,
+        out_shape=jax.ShapeDtypeStruct((owners, half, rows, feed_count), jnp.bfloat16),
+        in_specs=[in_vmem],
         out_specs=in_vmem,
-        scratch_shapes=[pltpu.VMEM((channels, rows, feed_count), jnp.bfloat16)],
         name="join",
-    )(*arrived)
-    spread = [joined] + [to_place(joined, k) for k in range(1, owners)]
+    )(arrived)
+    spread = lax.all_to_all(joined, "feed", 0, 0, axis_index_groups=planes, tiled=True)
     blocks = ROWS_DEV // BLOCK_ROWS
     return pl.pallas_call(
-        functools.partial(correlate_kernel, 1.0 / spectra_count, owners),
+        functools.partial(correlate_kernel, 1.0 / spectra_count),
         out_shape=jax.ShapeDtypeStruct((ROWS_DEV, 2 * total_feeds), jnp.float32),
-        in_specs=[in_vmem] * owners,
+        in_specs=[in_vmem],
         out_specs=pl.BlockSpec(memory_space=pl.ANY),
         scratch_shapes=[
-            pltpu.VMEM((owners, half, rows, feed_count), jnp.bfloat16),
             pltpu.VMEM((rows, total_feeds), jnp.bfloat16),
             pltpu.VMEM((blocks, 2 * BLOCK_ROWS, rows), jnp.bfloat16),
             pltpu.VMEM((ROWS_DEV, 2 * total_feeds), jnp.float32),
@@ -231,7 +208,7 @@
         ],
         compiler_params=pltpu.CompilerParams(vmem_limit_bytes=32 * 2**20),
         name="correlate",
-    )(*spread)
+    )(spread)
 
 
 def solution(mesh):

time: 37.9 us -> 40.2 us (1.061)
  blocking collectives: 0 us -> 20.1 us
  starting transfers between devices: 8.76 us -> 0 us
  waiting for transfers between devices: 5.92 us -> 0 us
  Pallas kernels: 21.5 us -> 19.8 us
  local copies, waits for them, and re-layouts: 1.36 us -> 0 us
    all_to_all x0 -> x2, blocking collectives: none -> 20.1 us  [the longest x1 12.2 us: body(): lax.all_to_all(sent, 'feed', 0, 0, axis_index_groups=lines, tiled=True)]
    ppermute x6 -> x0, starting transfers between devices: 8.76 us -> none  [the longest x3 7.01 us: to_plane(): return lax.ppermute(value, 'feed', pairs)]
    ppermute x6 -> x0, waiting for transfers between devices: 5.92 us -> none  [the longest x3 3.32 us: to_place(): return lax.ppermute(value, 'feed', pairs)]
    pallas_call x3, Pallas kernels: 21.5 us -> 19.8 us  [the longest x1 14.5 us: body(): pl.pallas_call(functools.partial(spectra_kernel, owners), out_shape=jax.S...]
    unnamed x8 -> x0, local copies, waits for them, and re-layouts: 1.36 us -> none
  transfers between devices with their start and end apart: 6 -> 0, of which waited for: 5 -> 0; matrix products, arithmetic and copies ran while one was open for 0% -> 0% of each run, Pallas kernels for 0% -> 0%
where the time goes in v1:
time: 40.2 us; the launch traced here: 39.9 us
  blocking collectives  20.1 us (50%)
  Pallas kernels  19.8 us (49%)
    pallas_call x1, Pallas kernels, body(): pl.pallas_call(functools.partial(spectra_kernel, owners), out_shape=jax.S...  14.5 us
    all_to_all x1, blocking collectives, body(): lax.all_to_all(sent, 'feed', 0, 0, axis_index_groups=lines, tiled=True)  12.2 us
    all_to_all x1, blocking collectives, body(): lax.all_to_all(joined, 'feed', 0, 0, axis_index_groups=planes, tiled=True)  7.92 us
    pallas_call x1, Pallas kernels, body(): pl.pallas_call(functools.partial(correlate_kernel, 1.0 / spectra_count),...  3.79 us
    pallas_call x1, Pallas kernels, body(): pl.pallas_call(join_kernel, out_shape=jax.ShapeDtypeStruct((owners, half,...  1.51 us

profile of v1, /device:TPU:0, one launch (start us, length us, event | category | flops | bytes accessed | tf_op | source)
XLA Modules:
  0.0 39.9 jit_solution(10897133555610609513)
XLA Ops:
  0.0 14.5 %spectra.1 = bf16[4,32,256]{2,1,0:T(8,128)(2,1)} custom-call(bf16[1,256,65536]{2,1,0:T(8,128)(2,1)} %x_hbm.1, f32[4,8192]{1,0:T(4,128)} %taps_ref.1, f32[8,8192]{1,0:T(8,128)} %constant.2.clone.dft_ref), custom_call_target="tpu_custom_call" | custom-call | tf_op jit(solution)/shard_map/spectra/pallas_call | solution.py:170
  14.5 12.2 %all_to_all.10.slots = bf16[4,32,256]{2,1,0:T(8,128)(2,1)} all-to-all(bf16[4,32,256]{2,1,0:T(8,128)(2,1)} %spectra.1), channel_id=1, replica_groups={{0,4,8,12},{1,5,9,13},{2,6,10,14},{3,7,11,15},{16,20,24,28},{17,21,25,2..., dimensions={0} | all-to-all | bytes 131072 | tf_op jit(solution)/shard_map/all_to_all | solution.py:188
  26.6 1.5 %join.1 = bf16[4,2,32,256]{3,2,1,0:T(8,128)(2,1)} custom-call(bf16[4,32,256]{2,1,0:T(8,128)(2,1)} %all_to_all.10.slots), custom_call_target="tpu_custom_call" | custom-call | tf_op jit(solution)/shard_map/join/pallas_call | solution.py:189
  28.2 7.9 %all_to_all.11.got = bf16[4,2,32,256]{3,2,1,0:T(8,128)(2,1)S(1)} all-to-all(bf16[4,2,32,256]{3,2,1,0:T(8,128)(2,1)} %join.1), channel_id=1, replica_groups={{0,1,2,3},{4,5,6,7},{8,9,10,11},{12,13,14,15},{16,17,18,19},{20,21,22,2..., dimensions={0} | all-to-all | bytes 262144 | tf_op jit(solution)/shard_map/all_to_all | solution.py:196
  36.1 3.8 %correlate.1 = f32[512,4096]{1,0:T(8,128)} custom-call(bf16[4,2,32,256]{3,2,1,0:T(8,128)(2,1)S(1)} %all_to_all.11.got), custom_call_target="tpu_custom_call" | custom-call | tf_op jit(solution)/shard_map/correlate/pallas_call | solution.py:198

commit v2 on v1

--- a/solution.py
+++ b/solution.py
@@ -13,6 +13,7 @@
 TIME_BLOCKS = 2
 ROWS_DEV = 512
 PIECES = 2
+AHEAD = 2
 TABLE_STEP = 1024
 BLOCK_ROWS = 64
 
@@ -26,7 +27,7 @@
 
 
 def spectra_kernel(
-    owners, x_hbm, taps_ref, dft_ref, out_ref, x_buf, table, window, parts, sems
+    owners, x_hbm, taps_ref, dft_ref, out_ref, x_buf, table, raw, window, parts, sems
 ):
     channels = dft_ref.shape[0] // 2
     tap_count, fft_len = taps_ref.shape
@@ -42,8 +43,7 @@
         span = pl.ds(pl.multiple_of(index * piece, piece), piece)
         return pltpu.make_async_copy(x_hbm.at[0, :, span], x_buf.at[:, span], sems.at[index])
 
-    @pl.loop(0, frame_count * PIECES)
-    def _(index):
+    for index in range(AHEAD * PIECES):
         fetch(index).start()
 
     window[...] = jnp.zeros_like(window)
@@ -57,11 +57,26 @@
         both = jnp.concatenate([high, scaled - high], axis=0)
         table[span, :] = both.T.astype(jnp.bfloat16)
 
+    def fold(frame, total):
+        turned = total.T
+        summed = turned[:width] + turned[width:]
+        for m in range(tap_count):
+            window[frame + edge - m] += summed[m * columns : (m + 1) * columns]
+
+    raw[...] = jnp.zeros_like(raw)
+
     @pl.loop(0, frame_count)
     def _(frame):
-        total = None
         for p in range(PIECES):
             fetch(frame * PIECES + p).wait()
+
+        @pl.when(frame + AHEAD < frame_count)
+        def _():
+            for p in range(PIECES):
+                fetch((frame + AHEAD) * PIECES + p).start()
+
+        fold(jnp.maximum(frame - 1, 0), raw[...])
+        total = None
         for p in range(PIECES):
             start = pl.multiple_of(frame * fft_len + p * piece, piece)
             product = jnp.dot(
@@ -70,10 +85,9 @@
                 preferred_element_type=jnp.float32,
             )
             total = product if total is None else total + product
-        turned = total.T
-        summed = turned[:width] + turned[width:]
-        for m in range(tap_count):
-            window[frame + edge - m] += summed[m * columns : (m + 1) * columns]
+        raw[...] = total
+
+    fold(frame_count - 1, raw[...])
 
     for spot in range(frame_count + edge):
         parts[:, spot, :] = window[spot]
@@ -97,13 +111,22 @@
         out_ref[c] = jnp.concatenate([high, extra], axis=0)
 
 
-def join_kernel(slots, out_ref):
-    channels, rows, feed_count = slots.shape
+def correlate_kernel(scale, owners, got_hbm, out_hbm, got, right, left, out_buf, got_sem, sems):
+    devices, rows, feed_count = got.shape
+    group_span = devices // TIME_BLOCKS
     frame_count = rows // 4
-    half = channels // TIME_BLOCKS
-    for p in range(half):
-        first = slots[p].astype(jnp.float32)
-        second = slots[half + p].astype(jnp.float32)
+    total_feeds = right.shape[1]
+    blocks = left.shape[0]
+    block_rows = left.shape[1] // 2
+    my_place = lax.axis_index("feed") % owners
+    load = pltpu.make_async_copy(got_hbm.at[:, lax.axis_index("feed") // owners], got, got_sem)
+    load.start()
+    load.wait()
+
+    for g in range(group_span):
+        span = slice(g * feed_count, (g + 1) * feed_count)
+        first = got[g].astype(jnp.float32)
+        second = got[group_span + g].astype(jnp.float32)
         extra = (
             first[2 * frame_count : 3 * frame_count]
             + first[3 * frame_count :]
@@ -112,23 +135,8 @@
         zero = jnp.zeros((frame_count - 4, feed_count), jnp.float32)
         extra = jnp.concatenate([extra[:4], zero, extra[4:8], zero], axis=0)
         fixed = second[: 2 * frame_count] + extra
-        for o in range(out_ref.shape[0]):
-            out_ref[o, p, : 2 * frame_count] = slots[p, : 2 * frame_count]
-            out_ref[o, p, 2 * frame_count :] = fixed.astype(jnp.bfloat16)
-
-
-def correlate_kernel(scale, got, out_hbm, right, left, out_buf, sems):
-    owners, half, rows, feed_count = got.shape
-    frame_count = rows // 4
-    total_feeds = right.shape[1]
-    blocks = left.shape[0]
-    block_rows = left.shape[1] // 2
-    my_place = lax.axis_index("feed") % owners
-
-    for o in range(owners):
-        for p in range(half):
-            start = (p * owners + o) * feed_count
-            right[:, start : start + feed_count] = got[o, p]
+        right[: 2 * frame_count, span] = got[g, : 2 * frame_count]
+        right[2 * frame_count :, span] = fixed.astype(jnp.bfloat16)
     row_start = my_place * ROWS_DEV
     mine = right[:, pl.ds(pl.multiple_of(row_start, ROWS_DEV), ROWS_DEV)].astype(jnp.float32)
     halves = [mine[k * frame_count : (k + 1) * frame_count] for k in range(4)]
@@ -175,6 +183,7 @@
         scratch_shapes=[
             pltpu.VMEM((feed_count, samples.shape[2]), jnp.bfloat16),
             pltpu.VMEM((fft_len, 2 * tap_count * columns), jnp.bfloat16),
+            pltpu.VMEM((feed_count, 2 * tap_count * columns), jnp.float32),
             pltpu.VMEM((frame_count + tap_count - 1, columns, feed_count), jnp.float32),
             pltpu.VMEM((columns, 2 * frame_count, feed_count), jnp.float32),
             pltpu.SemaphoreType.DMA((frame_count * PIECES,)),
@@ -183,30 +192,22 @@
         name="spectra",
     )(samples, pfb_taps, dft)
 
-    lines = [[z * owners + q for z in range(channels)] for q in range(owners)]
-    planes = [[z * owners + q for q in range(owners)] for z in range(channels)]
-    arrived = lax.all_to_all(sent, "feed", 0, 0, axis_index_groups=lines, tiled=True)
-    joined = pl.pallas_call(
-        join_kernel,
-        out_shape=jax.ShapeDtypeStruct((owners, half, rows, feed_count), jnp.bfloat16),
-        in_specs=[in_vmem],
-        out_specs=in_vmem,
-        name="join",
-    )(arrived)
-    spread = lax.all_to_all(joined, "feed", 0, 0, axis_index_groups=planes, tiled=True)
+    spread = lax.all_gather(sent, "feed", axis=0, tiled=False)
     blocks = ROWS_DEV // BLOCK_ROWS
     return pl.pallas_call(
-        functools.partial(correlate_kernel, 1.0 / spectra_count),
+        functools.partial(correlate_kernel, 1.0 / spectra_count, owners),
         out_shape=jax.ShapeDtypeStruct((ROWS_DEV, 2 * total_feeds), jnp.float32),
-        in_specs=[in_vmem],
+        in_specs=[pl.BlockSpec(memory_space=pl.ANY)],
         out_specs=pl.BlockSpec(memory_space=pl.ANY),
         scratch_shapes=[
+            pltpu.VMEM((devices, rows, feed_count), jnp.bfloat16),
             pltpu.VMEM((rows, total_feeds), jnp.bfloat16),
             pltpu.VMEM((blocks, 2 * BLOCK_ROWS, rows), jnp.bfloat16),
             pltpu.VMEM((ROWS_DEV, 2 * total_feeds), jnp.float32),
+            pltpu.SemaphoreType.DMA,
             pltpu.SemaphoreType.DMA((blocks,)),
         ],
-        compiler_params=pltpu.CompilerParams(vmem_limit_bytes=32 * 2**20),
+        compiler_params=pltpu.CompilerParams(vmem_limit_bytes=60 * 2**20),
         name="correlate",
     )(spread)
 

time: 40.2 us -> 73.4 us (1.83)
  waiting for transfers between devices: 0 us -> 40.8 us
  blocking collectives: 20.1 us -> 0 us
  between operations: 0.01 us -> 13.4 us
  Pallas kernels: 19.8 us -> 19 us
    all_gather x0 -> x1, waiting for transfers between devices: none -> 40.8 us  [body(): spread = lax.all_gather(sent, 'feed', axis=0, tiled=False)]
    all_to_all x2 -> x0, blocking collectives: 20.1 us -> none  [the longest x1 12.2 us: body(): lax.all_to_all(sent, 'feed', 0, 0, axis_index_groups=lines, tiled=True)]
    pallas_call x2 -> x1, Pallas kernels: 5.29 us -> 4.75 us  [body(): pl.pallas_call(functools.partial(correlate_kernel, 1.0 / spectra_count, o...]
  transfers between devices with their start and end apart: 0 -> 1, of which waited for: 0 -> 1; matrix products, arithmetic and copies ran while one was open for 0% -> 0% of each run, Pallas kernels for 0% -> 0%
where the time goes in v2:
time: 73.4 us; the launch traced here: 73.3 us
  waiting for transfers between devices  40.8 us (56%)
  Pallas kernels  19 us (26%)
  between operations  13.4 us (18%)
    all_gather x1, waiting for transfers between devices, body(): spread = lax.all_gather(sent, 'feed', axis=0, tiled=False)  40.8 us
    pallas_call x1, Pallas kernels, body(): pl.pallas_call(functools.partial(spectra_kernel, owners), out_shape=jax.S...  14.3 us
    pallas_call x1, Pallas kernels, body(): pl.pallas_call(functools.partial(correlate_kernel, 1.0 / spectra_count, o...  4.75 us
  transfers between devices with their start and end apart: 1, of which 1 were waited for; matrix products, arithmetic and copies ran while one was open for 0% of the time, Pallas kernels for 0%

profile of v2, /device:TPU:0, one launch (start us, length us, event | category | flops | bytes accessed | tf_op | source)
XLA Modules:
  0.0 73.3 jit_solution(14672877483908035127)
XLA Ops:
  6.5 0.0 all-gather.3.cloned.1.call-start
  6.5 14.3 %spectra.1 = bf16[4,32,256]{2,1,0:T(8,128)(2,1)} custom-call(bf16[1,256,65536]{2,1,0:T(8,128)(2,1)} %x_hbm.1, f32[4,8192]{1,0:T(4,128)} %taps_ref.1, f32[8,8192]{1,0:T(8,128)} %constant.2.clone.dft_ref), custom_call_target="tpu_custom_call" | custom-call | tf_op jit(solution)/shard_map/spectra/pallas_call | solution.py:178
  20.8 0.0 all-gather.3.cloned.1.call-update
  20.9 40.8 %all-gather.3.cloned.1.call-done = bf16[64,32,256]{2,1,0:T(8,128)(2,1)} async-done(((bf16[4,32,256]{2,1,0:T(8,128)(2,1)}), bf16[64,32,256]{2,1,0:T(8,128)(2,1)}) %all-gather.3.cloned.1.call-update) | async-done | bytes 1048592 | tf_op jit(solution)/shard_map/all_gather | solution.py:195
  61.6 4.8 %correlate.1 = f32[512,4096]{1,0:T(8,128)} custom-call(bf16[16,4,32,256]{3,2,1,0:T(8,128)(2,1)} %bitcast.1), custom_call_target="tpu_custom_call" | custom-call | tf_op jit(solution)/shard_map/correlate/pallas_call | solution.py:197
Async XLA Ops:
  6.5 55.1 %all-gather.3.cloned.1.call-start = ((), (), s32[]{:S(2)}) async-start(), calls=%async_computation | async-start | bytes 1114112 | tf_op jit(solution)/shard_map/all_gather | solution.py:195
Sparse Core Ops, SparseCore 0:
  21.0 40.6 all-gather.2

commit v3 on v0

--- a/solution.py
+++ b/solution.py
@@ -25,11 +25,12 @@
     return np.concatenate([np.cos(angle), -np.sin(angle)], axis=0).astype(np.float32)
 
 
-def spectra_kernel(owners, x_hbm, taps_ref, dft_ref, *rest):
-    channels = dft_ref.shape[0] // 2
-    outs, (x_buf, table, window, parts, sems) = rest[:channels], rest[channels:]
+def spectra_kernel(owners, x_hbm, taps_hbm, dft_hbm, *rest):
+    channels = dft_hbm.shape[0] // 2
+    outs, (taps_ref, dft_ref, x_buf, table, parts, small_sems, sems) = rest[:channels], rest[channels:]
     tap_count, fft_len = taps_ref.shape
     columns = 2 * channels
+    feed_count = x_hbm.shape[1]
     frame_count = x_hbm.shape[2] // fft_len
     piece = fft_len // PIECES
     edge = tap_count - 1
@@ -37,15 +38,24 @@
     my_plane = lax.axis_index("feed") // owners
     later_block = my_plane >= channels // TIME_BLOCKS
 
-    def fetch(index):
-        span = pl.ds(pl.multiple_of(index * piece, piece), piece)
-        return pltpu.make_async_copy(x_hbm.at[0, :, span], x_buf.at[:, span], sems.at[index])
-
-    @pl.loop(0, frame_count * PIECES)
-    def _(index):
-        fetch(index).start()
-
-    window[...] = jnp.zeros_like(window)
+    def fetch(frame):
+        source = pl.ds(pl.multiple_of(frame * fft_len, fft_len), fft_len)
+        rows = pl.ds(pl.multiple_of(frame * feed_count, feed_count), feed_count)
+        return pltpu.make_async_copy(x_hbm.at[0, :, source], x_buf.at[rows], sems.at[frame])
+
+    small = [
+        pltpu.make_async_copy(taps_hbm, taps_ref, small_sems.at[0]),
+        pltpu.make_async_copy(dft_hbm, dft_ref, small_sems.at[1]),
+    ]
+    for copy in small:
+        copy.start()
+
+    @pl.loop(0, frame_count)
+    def _(frame):
+        fetch(frame).start()
+
+    for copy in small:
+        copy.wait()
 
     @pl.loop(0, fft_len // TABLE_STEP)
     def _(index):
@@ -56,28 +66,41 @@
         both = jnp.concatenate([high, scaled - high], axis=0)
         table[span, :] = both.T.astype(jnp.bfloat16)
 
-    @pl.loop(0, frame_count)
-    def _(frame):
+    window = [None] * (frame_count + edge)
+
+    def fold(first, total):
+        for k in range(total.shape[0] // feed_count):
+            turned = total[k * feed_count : (k + 1) * feed_count].T
+            summed = turned[:width] + turned[width:]
+            for m in range(tap_count):
+                term = summed[m * columns : (m + 1) * columns]
+                spot = first + k + edge - m
+                window[spot] = term if window[spot] is None else window[spot] + term
+
+    before = None
+    starts = [0, *range(1, frame_count - 1, 2), frame_count - 1, frame_count]
+    for first, last in zip(starts[:-1], starts[1:]):
+        for frame in range(first, last):
+            fetch(frame).wait()
         total = None
         for p in range(PIECES):
-            fetch(frame * PIECES + p).wait()
-            start = pl.multiple_of(frame * fft_len + p * piece, piece)
+            span = slice(p * piece, (p + 1) * piece)
             product = jnp.dot(
-                x_buf[:, pl.ds(start, piece)],
-                table[p * piece : (p + 1) * piece, :],
+                x_buf[first * feed_count : last * feed_count, span],
+                table[span, :],
                 preferred_element_type=jnp.float32,
             )
             total = product if total is None else total + product
-        turned = total.T
-        summed = turned[:width] + turned[width:]
-        for m in range(tap_count):
-            window[frame + edge - m] += summed[m * columns : (m + 1) * columns]
+        if before is not None:
+            fold(*before)
+        before = (first, total)
+    fold(*before)
 
     for spot in range(frame_count + edge):
         parts[:, spot, :] = window[spot]
 
     for k in range(channels):
-        c = lax.rem(my_plane + k, channels)
+        c = lax.bitwise_xor(my_plane, k)
         now = jnp.concatenate([parts[c, :frame_count], parts[channels + c, :frame_count]], axis=0)
         high = now.astype(jnp.bfloat16)
         low = now - high.astype(jnp.float32)
@@ -105,7 +128,7 @@
     half = channels // TIME_BLOCKS
     my_plane = lax.axis_index("feed") // owners
     for k in range(channels):
-        slots[lax.rem(my_plane + channels - k, channels)] = refs[k][...]
+        slots[lax.bitwise_xor(my_plane, k)] = refs[k][...]
     for p in range(half):
         first = slots[p].astype(jnp.float32)
         second = slots[half + p].astype(jnp.float32)
@@ -131,7 +154,7 @@
     my_place = lax.axis_index("feed") % owners
 
     for k in range(owners):
-        slots[lax.rem(my_place + owners - k, owners)] = got[k][...]
+        slots[lax.bitwise_xor(my_place, k)] = got[k][...]
     for o in range(owners):
         for p in range(half):
             start = (p * owners + o) * feed_count
@@ -177,36 +200,32 @@
     sent = pl.pallas_call(
         functools.partial(spectra_kernel, owners),
         out_shape=[jax.ShapeDtypeStruct((rows, feed_count), jnp.bfloat16)] * channels,
-        in_specs=[pl.BlockSpec(memory_space=pl.ANY), in_vmem, in_vmem],
+        in_specs=[pl.BlockSpec(memory_space=pl.ANY)] * 3,
         out_specs=[in_vmem] * channels,
         scratch_shapes=[
-            pltpu.VMEM((feed_count, samples.shape[2]), jnp.bfloat16),
+            pltpu.VMEM(pfb_taps.shape, jnp.float32),
+            pltpu.VMEM(dft.shape, jnp.float32),
+            pltpu.VMEM((frame_count * feed_count, fft_len), jnp.bfloat16),
             pltpu.VMEM((fft_len, 2 * tap_count * columns), jnp.bfloat16),
-            pltpu.VMEM((frame_count + tap_count - 1, columns, feed_count), jnp.float32),
             pltpu.VMEM((columns, 2 * frame_count, feed_count), jnp.float32),
-            pltpu.SemaphoreType.DMA((frame_count * PIECES,)),
+            pltpu.SemaphoreType.DMA((2,)),
+            pltpu.SemaphoreType.DMA((frame_count,)),
         ],
-        compiler_params=pltpu.CompilerParams(vmem_limit_bytes=56 * 2**20),
+        compiler_params=pltpu.CompilerParams(vmem_limit_bytes=55200 * 2**10),
         name="spectra",
     )(samples, pfb_taps, dft)
 
-    def to_plane(value, k):
-        pairs = [
-            (z * owners + q, (z + k) % channels * owners + q)
-            for z in range(channels)
-            for q in range(owners)
-        ]
-        return lax.ppermute(value, "feed", pairs)
-
-    def to_place(value, k):
-        pairs = [
-            (z * owners + q, z * owners + (q + k) % owners)
-            for z in range(channels)
-            for q in range(owners)
-        ]
-        return lax.ppermute(value, "feed", pairs)
-
-    arrived = [sent[0]] + [to_plane(sent[k], k) for k in range(1, channels)]
+    def swap(value, bit):
+        return lax.ppermute(value, "feed", [(d, d ^ bit) for d in range(devices)])
+
+    held = {k: {0: sent[k]} for k in range(channels)}
+    bit = channels // 2
+    while bit:
+        for k in range(bit, 2 * bit):
+            for origin in sorted(held[k]):
+                held[k ^ bit][origin ^ bit] = swap(held[k][origin], bit * owners)
+        bit //= 2
+    arrived = [held[0][k] for k in range(channels)]
     joined = pl.pallas_call(
         functools.partial(join_kernel, owners),
         out_shape=jax.ShapeDtypeStruct((half, rows, feed_count), jnp.bfloat16),
@@ -215,7 +234,12 @@
         scratch_shapes=[pltpu.VMEM((channels, rows, feed_count), jnp.bfloat16)],
         name="join",
     )(*arrived)
-    spread = [joined] + [to_place(joined, k) for k in range(1, owners)]
+    spread = {0: joined}
+    bit = owners // 2
+    while bit:
+        for k in sorted(spread):
+            spread[k ^ bit] = swap(spread[k], bit)
+        bit //= 2
     blocks = ROWS_DEV // BLOCK_ROWS
     return pl.pallas_call(
         functools.partial(correlate_kernel, 1.0 / spectra_count, owners),
@@ -229,9 +253,9 @@
             pltpu.VMEM((ROWS_DEV, 2 * total_feeds), jnp.float32),
             pltpu.SemaphoreType.DMA((blocks,)),
         ],
-        compiler_params=pltpu.CompilerParams(vmem_limit_bytes=32 * 2**20),
+        compiler_params=pltpu.CompilerParams(vmem_limit_bytes=24 * 2**20),
         name="correlate",
-    )(*spread)
+    )(*[spread[k] for k in range(owners)])
 
 
 def solution(mesh):

time: 37.9 us -> 43.6 us (1.15)
  Pallas kernels: 21.5 us -> 25.4 us
  starting transfers between devices: 8.76 us -> 9.38 us
  local copies, waits for them, and re-layouts: 1.36 us -> 1.95 us
  waiting for transfers between devices: 5.92 us -> 6.47 us
    pallas_call x1, Pallas kernels: 16.3 us -> 20.2 us  [body(): pl.pallas_call(functools.partial(spectra_kernel, owners), out_shape=[jax....]
    ppermute x6 -> x7, starting transfers between devices: 8.76 us -> 9.38 us  [swap(): return lax.ppermute(value, 'feed', [(d, d ^ bit) for d in range(devices)])]
    unnamed x8 -> x10, local copies, waits for them, and re-layouts: 1.36 us -> 1.95 us
    ppermute x6 -> x7, waiting for transfers between devices: 5.92 us -> 6.47 us  [swap(): return lax.ppermute(value, 'feed', [(d, d ^ bit) for d in range(devices)])]
  transfers between devices with their start and end apart: 6 -> 7, of which waited for: 5 -> 3; matrix products, arithmetic and copies ran while one was open for 0% -> 0% of each run, Pallas kernels for 0% -> 0%
where the time goes in v3:
time: 43.6 us; the launch traced here: 43.3 us
  Pallas kernels  25.4 us (58%)
  starting transfers between devices  9.38 us (22%)
  waiting for transfers between devices  6.47 us (15%)
  local copies, waits for them, and re-layouts  1.95 us (4%)
    pallas_call x1, Pallas kernels, body(): pl.pallas_call(functools.partial(spectra_kernel, owners), out_shape=[jax....  20.2 us
    ppermute x7, starting transfers between devices, swap(): return lax.ppermute(value, 'feed', [(d, d ^ bit) for d in range(devices)])  9.38 us
    ppermute x7, waiting for transfers between devices, swap(): return lax.ppermute(value, 'feed', [(d, d ^ bit) for d in range(devices)])  6.47 us
    pallas_call x1, Pallas kernels, body(): pl.pallas_call(functools.partial(correlate_kernel, 1.0 / spectra_count, o...  3.8 us
    unnamed x10, local copies, waits for them, and re-layouts  1.95 us
    pallas_call x1, Pallas kernels, body(): pl.pallas_call(functools.partial(join_kernel, owners), out_shape=jax.Shap...  1.4 us
  transfers between devices with their start and end apart: 7, of which 3 were waited for; matrix products, arithmetic and copies ran while one was open for 0% of the time, Pallas kernels for 0%

profile of v3, /device:TPU:0, one launch (start us, length us, event | category | flops | bytes accessed | tf_op | source)
XLA Modules:
  0.0 43.3 jit_solution(18276119667152513800)
XLA Ops:
  0.0 20.2 %spectra.1 = (bf16[32,256]{1,0:T(8,128)(2,1)S(1)}, bf16[32,256]{1,0:T(8,128)(2,1)S(1)}, bf16[32,256]{1,0:T(8,128)(2,1)}, bf16[32,256]{1,0:T(8,128)(2,1)}) custom-call(bf16[1,256,65536]{2,1,0:T(8,128)(2,1)} %x_hbm.1, f32[4,8192]{1,0:T(4,128)} %taps_hbm.1, f32[8,8192]{1,0:T(8,128)} %constant.2.clone.dft_hbm), custom_call_target="tpu_custom_call" | custom-call | tf_op jit(solution)/shard_map/spectra/pallas_call | solution.py:200
  20.2 0.0 copy-start.1
  20.2 0.6 %copy-done.1 = bf16[32,256]{1,0:T(8,128)(2,1)} copy-done((bf16[32,256]{1,0:T(8,128)(2,1)}, bf16[32,256]{1,0:T(8,128)(2,1)S(1)}, u32[]{:S(2)}) %copy-start.1) | copy-done | bytes 16408
  20.8 4.0 %collective-permute-start.2 = (bf16[32,256]{1,0:T(8,128)(2,1)}, bf16[32,256]{1,0:T(8,128)(2,1)S(1)}, u32[]{:S(2)}, u32[]{:S(2)}) collective-permute-start(bf16[32,256]{1,0:T(8,128)(2,1)} %get-tuple-element.12), channel_id=1, source_target_pairs={{0,8},{1,9},{2,10},{3,11},{4,12},{5,13},{6,14},{7,15},{8,0},{9,1},... | collective-permute-start | bytes 49160 | tf_op jit(solution)/shard_map/ppermute | solution.py:219
  24.9 1.6 %collective-permute-start = (bf16[32,256]{1,0:T(8,128)(2,1)S(1)}, bf16[32,256]{1,0:T(8,128)(2,1)S(1)}, u32[]{:S(2)}, u32[]{:S(2)}) collective-permute-start(bf16[32,256]{1,0:T(8,128)(2,1)S(1)} %get-tuple-element.10), channel_id=1, source_target_pairs={{0,4},{1,5},{2,6},{3,7},{4,0},{5,1},{6,2},{7,3},{8,12},{9,13},{10,... | collective-permute-start | bytes 49160 | tf_op jit(solution)/shard_map/ppermute | solution.py:219
  26.4 0.3 collective-permute-start.1
  26.8 0.0 collective-permute-done.2
  26.8 1.9 %collective-permute-start.3 = (bf16[32,256]{1,0:T(8,128)(2,1)S(1)}, bf16[32,256]{1,0:T(8,128)(2,1)S(1)}, u32[]{:S(2)}, u32[]{:S(2)}) collective-permute-start(bf16[32,256]{1,0:T(8,128)(2,1)S(1)} %collective-permute-done.2), channel_id=1, source_target_pairs={{0,4},{1,5},{2,6},{3,7},{4,0},{5,1},{6,2},{7,3},{8,12},{9,13},{10,... | collective-permute-start | bytes 49160 | tf_op jit(solution)/shard_map/ppermute | solution.py:219
  28.7 0.0 collective-permute-done.refs_1_
  28.7 0.0 copy-start.2
  28.7 2.6 %collective-permute-done.1.refs_2_ = bf16[32,256]{1,0:T(8,128)(2,1)S(1)} collective-permute-done((bf16[32,256]{1,0:T(8,128)(2,1)}, bf16[32,256]{1,0:T(8,128)(2,1)S(1)}, u32[]{:S(2)}, u32[]{:S(2)}) %collective-permute-start.1) | collective-permute-done | bytes 16416 | tf_op jit(solution)/shard_map/ppermute | solution.py:219
  31.4 0.0 copy-start.3
  31.4 0.0 collective-permute-done.3.refs_3_
  31.4 0.0 copy-start.4
  31.4 0.0 copy-done.2
  31.4 0.6 %copy-done.3 = bf16[32,256]{1,0:T(8,128)(2,1)} copy-done((bf16[32,256]{1,0:T(8,128)(2,1)}, bf16[32,256]{1,0:T(8,128)(2,1)S(1)}, u32[]{:S(2)}) %copy-start.3) | copy-done | bytes 16408
  32.0 0.0 copy-done.4
  32.0 1.4 %join.1.refs_0_ = bf16[2,32,256]{2,1,0:T(8,128)(2,1)} custom-call(bf16[32,256]{1,0:T(8,128)(2,1)} %copy-done.1, bf16[32,256]{1,0:T(8,128)(2,1)} %copy-done.2, bf16[32,256]{1,0:T(8,128)(2,1)} %copy-done.3, bf16[32,256]{1,0:T(8,128)(2,1)} %copy-done.4), custom_call_target="tpu_custom_call" | custom-call | tf_op jit(solution)/shard_map/join/pallas_call | solution.py:229
  33.4 1.5 %collective-permute-start.5 = (bf16[2,32,256]{2,1,0:T(8,128)(2,1)}, bf16[2,32,256]{2,1,0:T(8,128)(2,1)S(1)}, u32[]{:S(2)}, u32[]{:S(2)}) collective-permute-start(bf16[2,32,256]{2,1,0:T(8,128)(2,1)} %join.1.refs_0_), channel_id=1, source_target_pairs={{0,2},{1,3},{2,0},{3,1},{4,6},{5,7},{6,4},{7,5},{8,10},{9,11},{10,... | collective-permute-start | bytes 98312 | tf_op jit(solution)/shard_map/ppermute | solution.py:219
  34.9 0.0 collective-permute-start.4
  34.9 2.6 %collective-permute-done.5.refs_2_ = bf16[2,32,256]{2,1,0:T(8,128)(2,1)S(1)} collective-permute-done((bf16[2,32,256]{2,1,0:T(8,128)(2,1)}, bf16[2,32,256]{2,1,0:T(8,128)(2,1)S(1)}, u32[]{:S(2)}, u32[]{:S(2)}) %collective-permute-start.5) | collective-permute-done | bytes 32800 | tf_op jit(solution)/shard_map/ppermute | solution.py:219
  37.5 0.0 collective-permute-start.6
  37.5 0.0 collective-permute-done.4.refs_1_
  37.5 1.2 %collective-permute-done.6.refs_3_ = bf16[2,32,256]{2,1,0:T(8,128)(2,1)S(1)} collective-permute-done((bf16[2,32,256]{2,1,0:T(8,128)(2,1)S(1)}, bf16[2,32,256]{2,1,0:T(8,128)(2,1)S(1)}, u32[]{:S(2)}, u32[]{:S(2)}) %collective-permute-start.6) | collective-permute-done | bytes 32800 | tf_op jit(solution)/shard_map/ppermute | solution.py:219
  38.7 0.0 copy-start
  38.7 0.8 %copy-done = bf16[2,32,256]{2,1,0:T(8,128)(2,1)S(1)} copy-done((bf16[2,32,256]{2,1,0:T(8,128)(2,1)S(1)}, bf16[2,32,256]{2,1,0:T(8,128)(2,1)}, u32[]{:S(2)}) %copy-start) | copy-done | bytes 32792
  39.5 3.8 %correlate.1 = f32[512,4096]{1,0:T(8,128)} custom-call(bf16[2,32,256]{2,1,0:T(8,128)(2,1)S(1)} %copy-done, bf16[2,32,256]{2,1,0:T(8,128)(2,1)S(1)} %collective-permute-done.4.refs_1_, bf16[2,32,256]{2,1,0:T(8,128)(2,1)S(1)} %collective-permute-done.5.refs_2_, bf16[2,32,256]{2,1,0:T(8,128)(2,1)S(1)} %collective-permute-done.6.refs_3_), custom_call_target="tpu_custom_call" | custom-call | tf_op jit(solution)/shard_map/correlate/pallas_call | solution.py:244
Async XLA Ops:
  20.2 0.6 %copy-start.1 = (bf16[32,256]{1,0:T(8,128)(2,1)}, bf16[32,256]{1,0:T(8,128)(2,1)S(1)}, u32[]{:S(2)}) copy-start(bf16[32,256]{1,0:T(8,128)(2,1)S(1)} %get-tuple-element.9.refs_0_) | copy-start | bytes 49156
  20.8 6.0 %collective-permute-start.2 = (bf16[32,256]{1,0:T(8,128)(2,1)}, bf16[32,256]{1,0:T(8,128)(2,1)S(1)}, u32[]{:S(2)}, u32[]{:S(2)}) collective-permute-start(bf16[32,256]{1,0:T(8,128)(2,1)} %get-tuple-element.12), channel_id=1, source_target_pairs={{0,8},{1,9},{2,10},{3,11},{4,12},{5,13},{6,14},{7,15},{8,0},{9,1},... | collective-permute-start | bytes 49160 | tf_op jit(solution)/shard_map/ppermute | solution.py:219
  24.9 3.9 %collective-permute-start = (bf16[32,256]{1,0:T(8,128)(2,1)S(1)}, bf16[32,256]{1,0:T(8,128)(2,1)S(1)}, u32[]{:S(2)}, u32[]{:S(2)}) collective-permute-start(bf16[32,256]{1,0:T(8,128)(2,1)S(1)} %get-tuple-element.10), channel_id=1, source_target_pairs={{0,4},{1,5},{2,6},{3,7},{4,0},{5,1},{6,2},{7,3},{8,12},{9,13},{10,... | collective-permute-start | bytes 49160 | tf_op jit(solution)/shard_map/ppermute | solution.py:219
  26.4 4.9 %collective-permute-start.1 = (bf16[32,256]{1,0:T(8,128)(2,1)}, bf16[32,256]{1,0:T(8,128)(2,1)S(1)}, u32[]{:S(2)}, u32[]{:S(2)}) collective-permute-start(bf16[32,256]{1,0:T(8,128)(2,1)} %get-tuple-element.11), channel_id=1, source_target_pairs={{0,8},{1,9},{2,10},{3,11},{4,12},{5,13},{6,14},{7,15},{8,0},{9,1},... | collective-permute-start | bytes 49160 | tf_op jit(solution)/shard_map/ppermute | solution.py:219
  26.8 4.6 %collective-permute-start.3 = (bf16[32,256]{1,0:T(8,128)(2,1)S(1)}, bf16[32,256]{1,0:T(8,128)(2,1)S(1)}, u32[]{:S(2)}, u32[]{:S(2)}) collective-permute-start(bf16[32,256]{1,0:T(8,128)(2,1)S(1)} %collective-permute-done.2), channel_id=1, source_target_pairs={{0,4},{1,5},{2,6},{3,7},{4,0},{5,1},{6,2},{7,3},{8,12},{9,13},{10,... | collective-permute-start | bytes 49160 | tf_op jit(solution)/shard_map/ppermute | solution.py:219
  28.7 2.6 %copy-start.2 = (bf16[32,256]{1,0:T(8,128)(2,1)}, bf16[32,256]{1,0:T(8,128)(2,1)S(1)}, u32[]{:S(2)}) copy-start(bf16[32,256]{1,0:T(8,128)(2,1)S(1)} %collective-permute-done.refs_1_) | copy-start | bytes 49156
  31.4 0.6 %copy-start.3 = (bf16[32,256]{1,0:T(8,128)(2,1)}, bf16[32,256]{1,0:T(8,128)(2,1)S(1)}, u32[]{:S(2)}) copy-start(bf16[32,256]{1,0:T(8,128)(2,1)S(1)} %collective-permute-done.1.refs_2_) | copy-start | bytes 49156
  31.4 0.6 %copy-start.4 = (bf16[32,256]{1,0:T(8,128)(2,1)}, bf16[32,256]{1,0:T(8,128)(2,1)S(1)}, u32[]{:S(2)}) copy-start(bf16[32,256]{1,0:T(8,128)(2,1)S(1)} %collective-permute-done.3.refs_3_) | copy-start | bytes 49156
  33.4 4.1 %collective-permute-start.5 = (bf16[2,32,256]{2,1,0:T(8,128)(2,1)}, bf16[2,32,256]{2,1,0:T(8,128)(2,1)S(1)}, u32[]{:S(2)}, u32[]{:S(2)}) collective-permute-start(bf16[2,32,256]{2,1,0:T(8,128)(2,1)} %join.1.refs_0_), channel_id=1, source_target_pairs={{0,2},{1,3},{2,0},{3,1},{4,6},{5,7},{6,4},{7,5},{8,10},{9,11},{10,... | collective-permute-start | bytes 98312 | tf_op jit(solution)/shard_map/ppermute | solution.py:219
  34.9 2.6 %collective-permute-start.4 = (bf16[2,32,256]{2,1,0:T(8,128)(2,1)}, bf16[2,32,256]{2,1,0:T(8,128)(2,1)S(1)}, u32[]{:S(2)}, u32[]{:S(2)}) collective-permute-start(bf16[2,32,256]{2,1,0:T(8,128)(2,1)} %join.1.refs_0_), channel_id=1, source_target_pairs={{0,1},{1,0},{2,3},{3,2},{4,5},{5,4},{6,7},{7,6},{8,9},{9,8},{10,11... | collective-permute-start | bytes 98312 | tf_op jit(solution)/shard_map/ppermute | solution.py:219
  37.5 1.2 %collective-permute-start.6 = (bf16[2,32,256]{2,1,0:T(8,128)(2,1)S(1)}, bf16[2,32,256]{2,1,0:T(8,128)(2,1)S(1)}, u32[]{:S(2)}, u32[]{:S(2)}) collective-permute-start(bf16[2,32,256]{2,1,0:T(8,128)(2,1)S(1)} %collective-permute-done.5.refs_2_), channel_id=1, source_target_pairs={{0,1},{1,0},{2,3},{3,2},{4,5},{5,4},{6,7},{7,6},{8,9},{9,8},{10,11... | collective-permute-start | bytes 98312 | tf_op jit(solution)/shard_map/ppermute | solution.py:219
  38.7 0.8 %copy-start = (bf16[2,32,256]{2,1,0:T(8,128)(2,1)S(1)}, bf16[2,32,256]{2,1,0:T(8,128)(2,1)}, u32[]{:S(2)}) copy-start(bf16[2,32,256]{2,1,0:T(8,128)(2,1)} %join.1.refs_0_) | copy-start | bytes 98308
